TPU v7x, 256 devices: a whole 4x4x8 slice. The times are simulated.
256 devices in a mesh: blk: 128 (over z, y, x_hi, core), grp: 2 (over x_lo).
Axes of the slice: x: 4 (x_hi: 2, x_lo: 2; x = x_hi * 2 + x_lo), y: 4, z: 8, core: 2. Of those that a mesh axis runs over, the one named last changes fastest.
Arguments:
- embeddings: bfloat16 [256, 2048, 768], P('blk', 'grp')
- counts: int32 [256], replicated, may hold values from 512 to 2048, as said below
- plan: int32 [128, 2], replicated, may hold values from 0 to 1
Outputs:
- density: float32 [256, 2048], P('blk', 'grp')
Inputs may be any that keep to these rules, and one draw needn't show every extreme that they name: `counts`: some block has exactly 2048 valid rows and some exactly 512.
All inputs are finite; a program needn't handle non-finite values.
Results may differ from a plain program's by a relative error of at most 0.0003.
Values may be sent and summed in bfloat16 or wider, within the bound.
A program may use at most 64 MiB of HBM per device.

v0:
```python
import jax
import jax.numpy as jnp
from jax import lax
from jax.sharding import PartitionSpec as P

kernel_scale = 4.0


def from_behind(block, axis, distance):
    devices = range(lax.axis_size(axis))
    route = [((i - distance) % len(devices), i) for i in devices]
    return lax.ppermute(block, axis, route)


def kernel_block(home_rows, home_norms, piece, guest_count):
    inner = lax.dot_general(
        home_rows, piece, (((1,), (1,)), ((), ())), preferred_element_type=jnp.float32
    )
    piece_norms = jnp.einsum("rd,rd->r", piece, piece, preferred_element_type=jnp.float32)
    column_ids = jnp.arange(piece.shape[0], dtype=jnp.int32)
    exponent = home_norms[:, None] + piece_norms[None, :] - 2.0 * inner
    values = jnp.exp(-kernel_scale * exponent)
    return jnp.where((column_ids < guest_count)[None, :], values, 0.0)


def on_device(embeddings, counts, plan):
    blocks_here = embeddings.shape[0]
    half_rows = embeddings.shape[1]
    own_index = lax.axis_index("blk")
    group_index = lax.axis_index("grp")
    blk_count = lax.axis_size("blk")
    norms = jnp.einsum("brd,brd->br", embeddings, embeddings, preferred_element_type=jnp.float32)
    own_rows = group_index * half_rows + jnp.arange(half_rows, dtype=jnp.int32)
    own_counts = lax.dynamic_slice_in_dim(counts, own_index * blocks_here, blocks_here, 0)
    own_valid = own_rows[None, :] < own_counts[:, None]
    slot_ids = jnp.arange(blocks_here, dtype=jnp.int32)
    density = jnp.zeros((blocks_here, half_rows), jnp.float32)
    for turn_index in range(plan.shape[1]):
        offset = turn_index + 1
        slot = plan[own_index, turn_index]
        home_rows = embeddings[slot]
        home_norms = norms[slot]
        home_valid = own_valid[slot]
        before_index = (own_index - offset) % blk_count
        before_count = counts[before_index * blocks_here + plan[before_index, turn_index]]
        incoming = from_behind(home_rows, "blk", offset)
        tile = kernel_block(
            home_rows, home_norms, lax.all_gather(incoming, "grp", axis=0, tiled=True), before_count
        )
        row_terms = jnp.sum(tile, axis=1)
        column_terms = jnp.sum(jnp.where(home_valid[:, None], tile, 0.0), axis=0)
        column_mine = lax.psum_scatter(column_terms, "grp", scatter_dimension=0, tiled=True)
        returned = from_behind(column_mine, "blk", -offset)
        update = row_terms + returned
        density = density + jnp.where((slot_ids == slot)[:, None], update[None, :], 0.0)
    return jnp.where(own_valid, density, 0.0)


def solution(mesh):
    return jax.shard_map(
        on_device,
        mesh=mesh,
        in_specs=(P("blk", "grp", None), P(), P()),
        out_specs=P("blk", "grp"),
        check_vma=False,
    )
```

profile of v0, /device:TPU:1, one launch (start us, length us, event | category | flops | bytes accessed | tf_op | source)
XLA Modules:
  0.0 201.4 jit_solution(4873907851765077845)
XLA Ops:
  6.5 0.0 all-gather.3.cloned.1.call-start
  6.5 1.5 constant_dynamic-slice_fusion.2
  11.9 3.3 %dynamic-slice_bitcast_fusion.1 = (bf16[1024,768]{1,0:T(8,128)(2,1)S(1)}, bf16[1024,768]{1,0:T(8,128)(2,1)}) fusion(bf16[2,1024,768]{2,1,0:T(8,128)(2,1)} %param.3, s32[]{:T(128)S(6)} %select_n.70, s32[]{:T(128)S(6)} %select_n.77), kind=kLoop, calls=%fused_computation.13 | loop fusion | bytes 6291464 | tf_op jit(solution)/shard_map/squeeze | solution.py:41
  15.2 0.0 copy-start.4
  15.2 0.0 copy-start.6
  15.2 0.0 copy-start.7
  15.2 0.0 copy-start
  15.2 1.2 copy-done.4
  16.4 4.1 %collective-permute-start = (bf16[1024,768]{1,0:T(8,128)(2,1)S(1)}, bf16[1024,768]{1,0:T(8,128)(2,1)}, u32[]{:S(2)}, u32[]{:S(2)}) collective-permute-start(bf16[1024,768]{1,0:T(8,128)(2,1)S(1)} %get-tuple-element.13), channel_id=1, source_target_pairs={{254,0},{0,2},{2,4},{4,6},{6,8},{8,10},{10,12},{12,14},{14,16},{16... | collective-permute-start | bytes 4718600 | tf_op jit(solution)/shard_map/ppermute | solution.py:12
  20.5 17.4 %collective-permute-done = bf16[1024,768]{1,0:T(8,128)(2,1)} collective-permute-done((bf16[1024,768]{1,0:T(8,128)(2,1)S(1)}, bf16[1024,768]{1,0:T(8,128)(2,1)}, u32[]{:S(2)}, u32[]{:S(2)}) %collective-permute-start) | collective-permute-done | bytes 1572896 | tf_op jit(solution)/shard_map/ppermute | solution.py:12
  37.8 0.0 all-gather.3.cloned.1.call-update
  37.9 0.0 all-gather.5.cloned.1.call-start
  37.9 1.3 collective-permute-start.2
  39.2 37.0 %collective-permute-done.2 = bf16[1024,768]{1,0:T(8,128)(2,1)} collective-permute-done((bf16[1024,768]{1,0:T(8,128)(2,1)}, bf16[1024,768]{1,0:T(8,128)(2,1)}, u32[]{:S(2)}, u32[]{:S(2)}) %collective-permute-start.2) | collective-permute-done | bytes 1572896 | tf_op jit(solution)/shard_map/ppermute | solution.py:12
  76.3 0.0 all-gather.5.cloned.1.call-update
  77.6 0.0 copy-done.6
  77.6 0.1 dynamic_slice.39
  77.7 0.0 copy-done.7
  77.7 0.6 dynamic-slice
  78.9 0.7 fusion.5
  79.6 0.1 broadcast_compare_fusion
  79.7 0.7 iota_compare_fusion.1
  80.3 0.6 iota_compare_fusion
  81.0 0.0 copy-done
  81.0 0.7 fusion.2
  81.7 27.8 %all-gather.3.cloned.1.call-done = bf16[2048,768]{1,0:T(8,128)(2,1)} async-done(((bf16[1024,768]{1,0:T(8,128)(2,1)}), bf16[2048,768]{1,0:T(8,128)(2,1)}) %all-gather.3.cloned.1.call-update) | async-done | bytes 3145744 | tf_op jit(solution)/shard_map/all_gather | solution.py:48
  109.5 0.0 copy-start.1
  109.5 2.7 %fusion.1 = f32[2048]{0:T(1024)S(1)} fusion(bf16[2048,768]{1,0:T(8,128)(2,1)} %all-gather.3.cloned.1.call-done), kind=kLoop, calls=%fused_computation.7 | loop fusion | flops 4716544 | bytes 3153920 | tf_op jit(solution)/shard_map/rd,rd->r/dot_general | solution.py:19
  112.2 52.1 %all-gather.5.cloned.1.call-done = bf16[2048,768]{1,0:T(8,128)(2,1)} async-done(((bf16[1024,768]{1,0:T(8,128)(2,1)}), bf16[2048,768]{1,0:T(8,128)(2,1)}) %all-gather.5.cloned.1.call-update) | async-done | bytes 3145744 | tf_op jit(solution)/shard_map/all_gather | solution.py:48
  164.4 0.0 copy-start.5
  164.4 2.7 %fusion = f32[2048]{0:T(1024)S(1)} fusion(bf16[2048,768]{1,0:T(8,128)(2,1)} %all-gather.5.cloned.1.call-done), kind=kLoop, calls=%fused_computation.5 | loop fusion | flops 4716544 | bytes 3153920 | tf_op jit(solution)/shard_map/rd,rd->r/dot_general | solution.py:19
  167.0 0.0 copy-done.1
  167.1 0.0 copy-done.5
  167.1 0.0 copy-start.2
  167.1 0.0 copy-start.3
  167.1 4.9 %select_reduce_fusion.1 = (f32[2048]{0:T(1024)S(1)}, f32[1024]{0:T(1024)S(1)}) fusion(f32[2048]{0:T(1024)S(1)} %fusion.1, f32[1024]{0:T(1024)S(1)} %bitcast.18, pred[1024]{0:T(1024)(128)(4,1)S(1)} %get-tuple-element.9, pred[2048]{0:T(1024)(128)(4,1)S(1)} %iota_compare_fusion.1, bf16[1024,768]{1,0:T(8,128)(2,1)S(1)} %copy-done.5, ...), kind=kOutput, calls=%fused_computation.2 | convolution fusion | flops 3237999616 | bytes 4746240 | tf_op jit(solution)/shard_map/dot_general | solution.py:16
  172.0 0.0 copy-done.2
  172.1 0.0 copy-done.3
  172.1 4.9 %select_reduce_fusion = (f32[2048]{0:T(1024)S(1)}, f32[1024]{0:T(1024)S(1)}) fusion(f32[2048]{0:T(1024)S(1)} %fusion, f32[1024]{0:T(1024)S(1)} %bitcast.17, pred[1024]{0:T(1024)(128)(4,1)S(1)} %get-tuple-element.10, pred[2048]{0:T(1024)(128)(4,1)S(1)} %iota_compare_fusion, bf16[1024,768]{1,0:T(8,128)(2,1)S(1)} %copy-done.3, bf16[2048,768]{1,0:T(8,128)(2,1)S(1)} %copy-done.2), kind=kOutput, calls=%fused_computation | convolution fusion | flops 3237999616 | bytes 4746240 | tf_op jit(solution)/shard_map/dot_general | solution.py:16
  177.0 5.3 %all-reduce.2 = (f32[2048]{0:T(1024)S(1)}, f32[2048]{0:T(1024)S(1)}) all-reduce(f32[2048]{0:T(1024)S(1)} %get-tuple-element.7, f32[2048]{0:T(1024)S(1)} %get-tuple-element.5), channel_id=3, replica_groups=mesh['blk'=128,'grp'=2] {'grp'}, use_global_device_ids=true, to_apply=%region_5.6.clone | all-reduce | flops 4096 | bytes 32768
  182.3 2.3 %collective-permute-start.1 = (f32[1024]{0:T(1024)S(1)}, f32[1024]{0:T(1024)S(1)}, u32[]{:S(2)}, u32[]{:S(2)}) collective-permute-start(f32[1024]{0:T(1024)S(1)} %dynamic-slice.1), channel_id=1, source_target_pairs={{2,0},{4,2},{6,4},{8,6},{10,8},{12,10},{14,12},{16,14},{18,16},{20... | collective-permute-start | bytes 12296 | tf_op jit(solution)/shard_map/ppermute | solution.py:12
  184.7 7.9 %collective-permute-start.3 = (f32[1024]{0:T(1024)S(1)}, f32[1024]{0:T(1024)S(1)}, u32[]{:S(2)}, u32[]{:S(2)}) collective-permute-start(f32[1024]{0:T(1024)S(1)} %dynamic-slice.3), channel_id=1, source_target_pairs={{4,0},{6,2},{8,4},{10,6},{12,8},{14,10},{16,12},{18,14},{20,16},{2... | collective-permute-start | bytes 12296 | tf_op jit(solution)/shard_map/ppermute | solution.py:12
  192.6 1.3 iota_compare_fusion.2
  193.8 0.0 collective-permute-done.1
  193.9 0.0 collective-permute-done.3
  193.9 0.7 add_select_fusion
  (7 shorter events, 0.1 us)
Async XLA Ops:
  6.5 102.9 %all-gather.3.cloned.1.call-start = ((), (), s32[]{:S(2)}) async-start(), calls=%async_computation | async-start | bytes 4718592 | tf_op jit(solution)/shard_map/all_gather | solution.py:48
  15.2 1.2 copy-start.4
  15.2 62.4 %copy-start.6 = (s32[256]{0:T(256)S(1)}, s32[256]{0:T(256)}, u32[]{:S(2)}) copy-start(s32[256]{0:T(256)} %param.4) | copy-start | bytes 3076
  15.2 62.5 %copy-start.7 = (u32[256]{0:T(256)S(1)}, u32[256]{0:T(256)}, u32[]{:S(2)}) copy-start(u32[256]{0:T(256)} %constant.50) | copy-start | bytes 3076
  15.2 65.8 %copy-start = (bf16[2,1024,768]{2,1,0:T(8,128)(2,1)S(1)}, bf16[2,1024,768]{2,1,0:T(8,128)(2,1)}, u32[]{:S(2)}) copy-start(bf16[2,1024,768]{2,1,0:T(8,128)(2,1)} %param.3) | copy-start | bytes 9437188
  16.4 21.4 %collective-permute-start = (bf16[1024,768]{1,0:T(8,128)(2,1)S(1)}, bf16[1024,768]{1,0:T(8,128)(2,1)}, u32[]{:S(2)}, u32[]{:S(2)}) collective-permute-start(bf16[1024,768]{1,0:T(8,128)(2,1)S(1)} %get-tuple-element.13), channel_id=1, source_target_pairs={{254,0},{0,2},{2,4},{4,6},{6,8},{8,10},{10,12},{12,14},{14,16},{16... | collective-permute-start | bytes 4718600 | tf_op jit(solution)/shard_map/ppermute | solution.py:12
  37.9 126.5 %all-gather.5.cloned.1.call-start = ((), (), s32[]{:S(2)}) async-start(), calls=%async_computation.1 | async-start | bytes 4718592 | tf_op jit(solution)/shard_map/all_gather | solution.py:48
  37.9 38.4 %collective-permute-start.2 = (bf16[1024,768]{1,0:T(8,128)(2,1)}, bf16[1024,768]{1,0:T(8,128)(2,1)}, u32[]{:S(2)}, u32[]{:S(2)}) collective-permute-start(bf16[1024,768]{1,0:T(8,128)(2,1)} %get-tuple-element.14), channel_id=1, source_target_pairs={{252,0},{254,2},{0,4},{2,6},{4,8},{6,10},{8,12},{10,14},{12,16},{1... | collective-permute-start | bytes 4718600 | tf_op jit(solution)/shard_map/ppermute | solution.py:12
  109.5 57.6 %copy-start.1 = (bf16[2048,768]{1,0:T(8,128)(2,1)S(1)}, bf16[2048,768]{1,0:T(8,128)(2,1)}, u32[]{:S(2)}) copy-start(bf16[2048,768]{1,0:T(8,128)(2,1)} %all-gather.3.cloned.1.call-done) | copy-start | bytes 9437188
  164.4 2.7 %copy-start.5 = (bf16[1024,768]{1,0:T(8,128)(2,1)S(1)}, bf16[1024,768]{1,0:T(8,128)(2,1)}, u32[]{:S(2)}) copy-start(bf16[1024,768]{1,0:T(8,128)(2,1)} %copy-done.4) | copy-start | bytes 4718596
  167.1 5.0 %copy-start.2 = (bf16[2048,768]{1,0:T(8,128)(2,1)S(1)}, bf16[2048,768]{1,0:T(8,128)(2,1)}, u32[]{:S(2)}) copy-start(bf16[2048,768]{1,0:T(8,128)(2,1)} %all-gather.5.cloned.1.call-done) | copy-start | bytes 9437188
  167.1 5.0 %copy-start.3 = (bf16[1024,768]{1,0:T(8,128)(2,1)S(1)}, bf16[1024,768]{1,0:T(8,128)(2,1)}, u32[]{:S(2)}) copy-start(bf16[1024,768]{1,0:T(8,128)(2,1)} %get-tuple-element.14) | copy-start | bytes 4718596
  182.3 11.5 %collective-permute-start.1 = (f32[1024]{0:T(1024)S(1)}, f32[1024]{0:T(1024)S(1)}, u32[]{:S(2)}, u32[]{:S(2)}) collective-permute-start(f32[1024]{0:T(1024)S(1)} %dynamic-slice.1), channel_id=1, source_target_pairs={{2,0},{4,2},{6,4},{8,6},{10,8},{12,10},{14,12},{16,14},{18,16},{20... | collective-permute-start | bytes 12296 | tf_op jit(solution)/shard_map/ppermute | solution.py:12
  184.7 9.2 %collective-permute-start.3 = (f32[1024]{0:T(1024)S(1)}, f32[1024]{0:T(1024)S(1)}, u32[]{:S(2)}, u32[]{:S(2)}) collective-permute-start(f32[1024]{0:T(1024)S(1)} %dynamic-slice.3), channel_id=1, source_target_pairs={{4,0},{6,2},{8,4},{10,6},{12,8},{14,10},{16,12},{18,14},{20,16},{2... | collective-permute-start | bytes 12296 | tf_op jit(solution)/shard_map/ppermute | solution.py:12
Sparse Core Ops, SparseCore 0:
  38.0 71.4 all-gather.2
  111.3 53.0 all-gather.4
where the time goes:
time: 202 us; the launch traced here: 201 us
  waiting for transfers between devices  134 us (66%)
  between operations  19.4 us (10%)
  starting transfers between devices  15.7 us (8%)
  matrix products  9.89 us (5%)
  other arithmetic  9.43 us (5%)
  local copies, waits for them, and re-layouts  7.4 us (4%)
  blocking collectives  5.3 us (3%)
    all_gather x2, waiting for transfers between devices, on_device(): lax.all_gather(incoming, 'grp', axis=0, tiled=True)  79.9 us
    ppermute x4, waiting for transfers between devices, from_behind(): return lax.ppermute(block, axis, route)  54.4 us
    ppermute x4, starting transfers between devices, from_behind(): return lax.ppermute(block, axis, route)  15.6 us
    dot_general x2, matrix products, kernel_block(): lax.dot_general(home_rows, piece, (((1,), (1,)), ((), ())), preferred_ele...  9.89 us
    dot_general x2, other arithmetic, kernel_block(): jnp.einsum('rd,rd->r', piece, piece, preferred_element_type=jnp.float32)  5.41 us
    unnamed x1, blocking collectives  5.3 us
  transfers between devices with their start and end apart: 6, of which 4 were waited for; matrix products, arithmetic and copies ran while one was open for 4% of the time, Pallas kernels for 0%

commit v1 on v0

v1 whole, which is shorter than its diff:
```python
import functools

import jax
import jax.numpy as jnp
from jax import lax
from jax.experimental import pallas as pl
from jax.experimental.pallas import tpu as pltpu
from jax.sharding import PartitionSpec as P

kernel_scale = 4.0
chunk = 128
mesh_id = pl.DeviceIdType.MESH


def lane_norms(rows, first_row, count):
    wide = rows.astype(jnp.float32)
    squares = wide * wide
    folded = squares[:, :128]
    for start in range(128, rows.shape[1], 128):
        folded = folded + squares[:, start : start + 128]
    norms = 0.5 * jnp.sum(folded.T, axis=0, keepdims=True)
    row_ids = first_row + lax.broadcasted_iota(jnp.int32, norms.shape, 1)
    return jnp.where(row_ids < count, norms, jnp.inf)


def column_norms(rows, first_row, count):
    wide = rows.astype(jnp.float32)
    norms = 0.5 * jnp.sum(wide * wide, axis=1, keepdims=True)
    row_ids = first_row + lax.broadcasted_iota(jnp.int32, norms.shape, 0)
    return jnp.where(row_ids < count, norms, jnp.inf)


def tile_sums(rows, norms, resident, resident_norms, totals):
    row_part = jnp.zeros((chunk, 128), jnp.float32)
    for start in range(0, resident.shape[0], 256):
        inner = lax.dot_general(
            rows, resident[start : start + 256, :], (((1,), (1,)), ((), ())), preferred_element_type=jnp.float32
        )
        for left in (0, 128):
            place = (start + left) // 128
            half_distance = (norms + resident_norms[place : place + 1, :]) - inner[:, left : left + 128]
            values = jnp.exp((-2.0 * kernel_scale) * half_distance)
            row_part = row_part + values
            totals[:, start + left : start + left + 128] += jnp.sum(values.reshape(chunk // 8, 8, 128), axis=0)
    return jnp.sum(row_part.T, axis=0, keepdims=True)


def folded_rows(totals):
    return jnp.concatenate(
        [jnp.sum(totals[:, k * 128 : (k + 1) * 128], axis=0, keepdims=True) for k in range(totals.shape[1] // 128)], axis=0
    )


def kernel(
    blk_count, plan, counts, embeddings, out,
    staged, played_0, played_1, mate_a, mate_b, guest_a, guest_b, chip_guest,
    norms, totals, sums, arrived,
    staged_sem, send_sem, recv_sem, sum_send_sem, sum_recv_sem,
):
    half_rows = embeddings.shape[1]
    chunks = half_rows // chunk
    m, g = lax.axis_index("blk"), lax.axis_index("grp")
    core = lax.rem(m, 2)
    back_1, back_2 = lax.rem(m + blk_count - 1, blk_count), lax.rem(m + blk_count - 2, blk_count)
    next_1, next_2 = lax.rem(m + 1, blk_count), lax.rem(m + 2, blk_count)
    mate, other_core = (m, 1 - g), (m + 1 - 2 * core, g)

    barrier = pltpu.get_barrier_semaphore()
    for device in (mate, (next_2, 1 - g), (back_2, 1 - g), (next_1, 1 - g), (back_1, 1 - g), other_core):
        pl.semaphore_signal(barrier, inc=1, device_id=device, device_id_type=mesh_id)

    def rows_of(k):
        return pl.ds(pl.multiple_of(k * chunk, chunk), chunk)

    def load(k):
        return pltpu.make_async_copy(embeddings.at[:, rows_of(k)], staged.at[:, rows_of(k)], staged_sem.at[k])

    for k in range(chunks):
        load(k).start()

    def copy(stream, source, target, device):
        def of(k):
            return pltpu.make_async_remote_copy(
                src_ref=source.at[rows_of(k)],
                dst_ref=target.at[rows_of(k)],
                send_sem=send_sem.at[stream, k],
                recv_sem=recv_sem.at[stream, k],
                device_id=device,
                device_id_type=mesh_id,
            )

        return of

    def sum_copy(source, target, device):
        return pltpu.make_async_remote_copy(
            src_ref=sums.at[source],
            dst_ref=arrived.at[target],
            send_sem=sum_send_sem.at[target],
            recv_sem=sum_recv_sem.at[target],
            device_id=device,
            device_id_type=mesh_id,
        )

    slot_0, slot_1 = plan[0, m], plan[1, m]
    count_0, count_1 = counts[2 * m + slot_0], counts[2 * m + slot_1]
    guest_count_0 = counts[2 * back_1 + plan[0, back_1]]
    guest_count_1 = counts[2 * back_2 + plan[1, back_2]]
    own_row, far_row = g * half_rows, (1 - g) * half_rows

    totals[...] = jnp.zeros_like(totals)

    to_mate_a0 = copy(0, played_0, mate_a, mate)
    to_mate_a1 = copy(0, played_1, mate_a, mate)
    to_mate_b = copy(1, played_1, mate_b, mate)
    to_next_a = copy(2, played_1, guest_a, (next_2, 1 - g))
    to_next_b = copy(3, played_0, guest_b, (next_1, 1 - g))
    to_core = copy(4, played_0, chip_guest.at[0], other_core)
    to_core_passed = copy(5, mate_a, chip_guest.at[1], other_core)

    pl.semaphore_wait(barrier, 6)
    for k in range(chunks):
        load(k).wait()
        here = rows_of(k)
        first, second = staged[0, here], staged[1, here]
        played_0[here, :] = jnp.where(slot_0 == 0, first, second)
        played_1[here, :] = jnp.where(slot_1 == 0, first, second)

        @pl.when(core == 0)
        def _():
            to_mate_a0(k).start()
            to_next_a(k).start()
            to_core(k).start()

        @pl.when(core == 1)
        def _():
            to_next_b(k).start()
            to_mate_a1(k).start()

    for k in range(chunks):

        @pl.when(core == 0)
        def _():
            to_mate_b(k).start()

        @pl.when(core == 1)
        def _():
            to_next_a(k).start()

    def own_norms(k, carry):
        here = rows_of(k)
        norms[0, pl.ds(k, 1), :] = lane_norms(played_0[here, :], own_row + k * chunk, count_0)
        norms[1, pl.ds(k, 1), :] = lane_norms(played_1[here, :], own_row + k * chunk, count_1)
        return carry

    lax.fori_loop(0, chunks, own_norms, 0)

    @pl.when(core == 0)
    def _():
        def while_arriving(k, carry):
            here = rows_of(k)
            to_mate_a0(k).wait_recv()
            to_core_passed(k).start()
            norms[2, pl.ds(k, 1), :] = lane_norms(mate_a[here, :], far_row + k * chunk, count_0)
            to_next_b(k).wait_recv()
            rows = guest_b[here, :]
            beside = column_norms(rows, far_row + k * chunk, guest_count_0)
            sums[0, pl.ds(k, 1), :] = tile_sums(rows, beside, played_0, norms.at[0], totals.at[0])
            to_next_a(k).wait_recv()
            rows = guest_a[here, :]
            norms[3, pl.ds(k, 1), :] = lane_norms(rows, far_row + k * chunk, guest_count_1)
            beside = column_norms(rows, far_row + k * chunk, guest_count_1)
            sums[1, pl.ds(k, 1), :] = tile_sums(rows, beside, played_1, norms.at[1], totals.at[1])
            return carry

        lax.fori_loop(0, chunks, while_arriving, 0)

        def round_0(k, carry):
            rows = guest_b[rows_of(k), :]
            beside = column_norms(rows, far_row + k * chunk, guest_count_0)
            sums[0, pl.ds(k, 1), :] += tile_sums(rows, beside, mate_a, norms.at[2], totals.at[2])
            return carry

        lax.fori_loop(0, chunks, round_0, 0)
        sums[2] = folded_rows(totals[2])
        sum_copy(0, 5, (back_1, 1 - g)).start()
        sum_copy(2, 0, mate).start()

        def round_1(k, carry):
            to_mate_b(k).wait_recv()
            rows = mate_b[rows_of(k), :]
            beside = column_norms(rows, far_row + k * chunk, count_1)
            sums[3, pl.ds(k, 1), :] = tile_sums(rows, beside, guest_a, norms.at[3], totals.at[3])
            return carry

        lax.fori_loop(0, chunks, round_1, 0)
        sum_copy(3, 1, mate).start()
        sums[1] += folded_rows(totals[3])
        sum_copy(1, 4, (back_2, 1 - g)).start()

    @pl.when(core == 1)
    def _():
        def near_half(k, carry):
            to_core(k).wait_recv()
            rows = chip_guest[0, rows_of(k), :]
            beside = column_norms(rows, own_row + k * chunk, guest_count_0)
            sums[0, pl.ds(k, 1), :] = tile_sums(rows, beside, played_0, norms.at[0], totals.at[0])
            return carry

        lax.fori_loop(0, chunks, near_half, 0)
        sum_copy(0, 2, other_core).start()

        def far_half(k, carry):
            here = rows_of(k)
            to_mate_a1(k).wait_recv()
            norms[2, pl.ds(k, 1), :] = lane_norms(mate_a[here, :], far_row + k * chunk, count_1)
            to_core_passed(k).wait_recv()
            rows = chip_guest[1, here, :]
            beside = column_norms(rows, far_row + k * chunk, guest_count_0)
            sums[1, pl.ds(k, 1), :] = tile_sums(rows, beside, played_0, norms.at[0], totals.at[0])
            return carry

        lax.fori_loop(0, chunks, far_half, 0)
        sum_copy(1, 3, (back_1, 1 - g)).start()

        def round_1(k, carry):
            to_next_a(k).wait_recv()
            rows = guest_a[rows_of(k), :]
            beside = column_norms(rows, far_row + k * chunk, guest_count_1)
            near = tile_sums(rows, beside, played_1, norms.at[1], totals.at[1])
            sums[2, pl.ds(k, 1), :] = near + tile_sums(rows, beside, mate_a, norms.at[2], totals.at[2])
            return carry

        lax.fori_loop(0, chunks, round_1, 0)
        sum_copy(2, 4, (back_2, 1 - g)).start()
        sums[3] = folded_rows(totals[2])
        sum_copy(3, 1, mate).start()

    def store(density_0, density_1):
        places = lax.broadcasted_iota(jnp.int32, (chunks, 128), 0) * 128 + lax.broadcasted_iota(jnp.int32, (chunks, 128), 1)
        for slot in range(2):
            both = jnp.where(slot_0 == slot, density_0, 0.0) + jnp.where(slot_1 == slot, density_1, 0.0)
            both = jnp.where(own_row + places < counts[2 * m + slot], both, 0.0)
            for k in range(chunks):
                out[slot : slot + 1, k * 128 : (k + 1) * 128] = both[k : k + 1, :]

    mine_0, mine_1 = folded_rows(totals[0]), folded_rows(totals[1])

    @pl.when(core == 0)
    def _():
        for target in (0, 1, 2, 3, 4):
            sum_copy(0, target, mate).wait_recv()
        store(mine_0 + arrived[0] + arrived[2] + arrived[3], mine_1 + arrived[1] + arrived[4])
        for k in range(chunks):
            for sent in (to_mate_a0, to_next_a, to_core, to_mate_b, to_core_passed):
                sent(k).wait_send()
        for source, target in ((0, 5), (2, 0), (3, 1), (1, 4)):
            sum_copy(source, target, mate).wait_send()

    @pl.when(core == 1)
    def _():
        for target in (1, 4, 5):
            sum_copy(0, target, mate).wait_recv()
        store(mine_0 + arrived[5], mine_1 + arrived[1] + arrived[4])
        for k in range(chunks):
            for sent in (to_mate_a1, to_next_a, to_next_b):
                sent(k).wait_send()
        for source, target in ((0, 2), (1, 3), (2, 4), (3, 1)):
            sum_copy(source, target, mate).wait_send()


def on_device(embeddings, counts, plan):
    _, half_rows, width = embeddings.shape
    chunks = half_rows // chunk
    half_block = pltpu.VMEM((half_rows, width), embeddings.dtype)
    two_halves = pltpu.VMEM((2, half_rows, width), embeddings.dtype)
    return pl.pallas_call(
        functools.partial(kernel, lax.axis_size("blk")),
        out_shape=jax.ShapeDtypeStruct((2, half_rows), jnp.float32),
        in_specs=[
            pl.BlockSpec(memory_space=pltpu.SMEM),
            pl.BlockSpec(memory_space=pltpu.SMEM),
            pl.BlockSpec(memory_space=pl.ANY),
        ],
        out_specs=pl.BlockSpec(memory_space=pltpu.VMEM),
        scratch_shapes=[
            two_halves,
            half_block, half_block, half_block, half_block, half_block, half_block,
            two_halves,
            pltpu.VMEM((4, chunks, 128), jnp.float32),
            pltpu.VMEM((4, 8, half_rows), jnp.float32),
            pltpu.VMEM((4, chunks, 128), jnp.float32),
            pltpu.VMEM((6, chunks, 128), jnp.float32),
            pltpu.SemaphoreType.DMA((chunks,)),
            pltpu.SemaphoreType.DMA((6, chunks)),
            pltpu.SemaphoreType.DMA((6, chunks)),
            pltpu.SemaphoreType.DMA((6,)),
            pltpu.SemaphoreType.DMA((6,)),
        ],
        compiler_params=pltpu.CompilerParams(
            collective_id=0, has_side_effects=True, vmem_limit_bytes=56 * 2**20
        ),
    )(plan.T, counts, embeddings)


def solution(mesh):
    return jax.shard_map(
        on_device,
        mesh=mesh,
        in_specs=(P("blk", "grp", None), P(), P()),
        out_specs=P("blk", "grp"),
        check_vma=False,
    )
```

time: 202 us -> 71.6 us (0.35)
  waiting for transfers between devices: 134 us -> 0 us
  Pallas kernels: 0 us -> 70.1 us
  between operations: 19.4 us -> 0.01 us
  starting transfers between devices: 15.7 us -> 0 us
  matrix products: 9.89 us -> 0 us
  other arithmetic: 9.43 us -> 0 us
  local copies, waits for them, and re-layouts: 7.4 us -> 1.3 us
  blocking collectives: 5.3 us -> 0 us
    all_gather x2 -> x0, waiting for transfers between devices: 79.9 us -> none  [on_device(): lax.all_gather(incoming, 'grp', axis=0, tiled=True)]
    pallas_call x0 -> x1, Pallas kernels: none -> 70.1 us  [on_device(): pl.pallas_call(functools.partial(kernel, lax.axis_size('blk')), out_shape...]
    ppermute x4 -> x0, waiting for transfers between devices: 54.4 us -> none  [from_behind(): return lax.ppermute(block, axis, route)]
    ppermute x4 -> x0, starting transfers between devices: 15.6 us -> none  [from_behind(): return lax.ppermute(block, axis, route)]
    dot_general x2 -> x0, matrix products: 9.89 us -> none  [kernel_block(): lax.dot_general(home_rows, piece, (((1,), (1,)), ((), ())), preferred_ele...]
    dot_general x3 -> x0, other arithmetic: 6.1 us -> none  [the longest x2 5.41 us: kernel_block(): jnp.einsum('rd,rd->r', piece, piece, preferred_element_type=jnp.float32)]
    unnamed x1 -> x0, blocking collectives: 5.3 us -> none
    squeeze x1 -> x0, local copies, waits for them, and re-layouts: 3.3 us -> none  [on_device(): home_rows = embeddings[slot]]
  transfers between devices with their start and end apart: 6 -> 0, of which waited for: 4 -> 0; matrix products, arithmetic and copies ran while one was open for 4% -> 0% of each run, Pallas kernels for 0% -> 0%
where the time goes in v1:
time: 71.6 us; the launch traced here: 71.4 us
  Pallas kernels  70.1 us (98%)
  local copies, waits for them, and re-layouts  1.3 us (2%)
    pallas_call x1, Pallas kernels, on_device(): pl.pallas_call(functools.partial(kernel, lax.axis_size('blk')), out_shape...  70.1 us

profile of v1, /device:TPU:1, one launch (start us, length us, event | category | flops | bytes accessed | tf_op | source)
XLA Modules:
  0.0 71.4 jit_solution(7842958151709994378)
XLA Ops:
  0.0 70.1 %shard_map.37 = f32[2,1024]{1,0:T(2,128)} custom-call(s32[2,128]{1,0:T(2,128)} %bitcast.1, s32[256]{0:T(256)} %counts.1, bf16[2,1024,768]{2,1,0:T(8,128)(2,1)} %embeddings.1), custom_call_target="tpu_custom_call" | custom-call | tf_op jit(solution)/shard_map/pallas_call | solution.py:276
  70.1 1.3 %copy.5 = f32[2,1024]{1,0:T(2,128)} copy(f32[2,1024]{1,0:T(2,128)} %shard_map.37) | data formatting | bytes 16384

commit v2 on v1

v2 whole, which is shorter than its diff:
```python
import functools

import jax
import jax.numpy as jnp
from jax import lax
from jax.experimental import pallas as pl
from jax.experimental.pallas import tpu as pltpu
from jax.sharding import PartitionSpec as P

kernel_scale = 4.0
chunk = 128
mesh_id = pl.DeviceIdType.MESH


def lane_norms(rows, first_row, count):
    wide = rows.astype(jnp.float32)
    squares = wide * wide
    folded = squares[:, :128]
    for start in range(128, rows.shape[1], 128):
        folded = folded + squares[:, start : start + 128]
    norms = 0.5 * jnp.sum(folded.T, axis=0, keepdims=True)
    row_ids = first_row + lax.broadcasted_iota(jnp.int32, norms.shape, 1)
    return jnp.where(row_ids < count, norms, jnp.inf)


def column_norms(rows, first_row, count):
    wide = rows.astype(jnp.float32)
    norms = 0.5 * jnp.sum(wide * wide, axis=1, keepdims=True)
    row_ids = first_row + lax.broadcasted_iota(jnp.int32, norms.shape, 0)
    return jnp.where(row_ids < count, norms, jnp.inf)


def tile_sums(rows, norms, resident, resident_norms, totals):
    height, width = rows.shape[0], 256
    row_part = jnp.zeros((height, 128), jnp.float32)
    for start in range(0, resident.shape[0], width):
        inner = lax.dot_general(
            rows, resident[start : start + width, :], (((1,), (1,)), ((), ())), preferred_element_type=jnp.float32
        )
        for left in range(0, width, 128):
            place = (start + left) // 128
            half_distance = (norms + resident_norms[place : place + 1, :]) - inner[:, left : left + 128]
            values = jnp.exp((-2.0 * kernel_scale) * half_distance)
            row_part = row_part + values
            totals[:, start + left : start + left + 128] += jnp.sum(values.reshape(height // 8, 8, 128), axis=0)
    return jnp.sum(row_part.T, axis=0, keepdims=True)


def folded_rows(totals):
    return jnp.concatenate(
        [jnp.sum(totals[:, k * 128 : (k + 1) * 128], axis=0, keepdims=True) for k in range(totals.shape[1] // 128)], axis=0
    )


def kernel(
    blk_count, plan_in_hbm, counts_in_hbm, embeddings, out,
    plan, counts, staged, played_0, played_1, mate_a, mate_b, guest_a, guest_b, chip_guest,
    norms, totals, sums, arrived,
    ready, turn, small_sem, staged_sem, send_sem, recv_sem, sum_send_sem, sum_recv_sem,
):
    half_rows = embeddings.shape[1]
    chunks = half_rows // chunk
    m, g = lax.axis_index("blk"), lax.axis_index("grp")
    core = lax.rem(m, 2)
    back_1, back_2 = lax.rem(m + blk_count - 1, blk_count), lax.rem(m + blk_count - 2, blk_count)
    next_1, next_2 = lax.rem(m + 1, blk_count), lax.rem(m + 2, blk_count)
    mate, other_core = (m, 1 - g), (m + 1 - 2 * core, g)

    barrier = pltpu.get_barrier_semaphore()
    sender = (back_1, lax.rem(1 - g + core, 2))
    for device in (mate, (back_2, 1 - g), sender):
        pl.semaphore_signal(barrier, inc=1, device_id=device, device_id_type=mesh_id)

    def rows_of(k):
        return pl.ds(pl.multiple_of(k * chunk, chunk), chunk)

    def load(k):
        return pltpu.make_async_copy(embeddings.at[:, rows_of(k)], staged.at[:, rows_of(k)], staged_sem.at[k])

    load_plan = pltpu.make_async_copy(plan_in_hbm, plan, small_sem.at[0])
    load_counts = pltpu.make_async_copy(counts_in_hbm, counts, small_sem.at[1])
    load_plan.start()
    load_counts.start()
    for k in range(chunks):
        load(k).start()

    def copy(stream, source, target, device):
        def of(k):
            return pltpu.make_async_remote_copy(
                src_ref=source.at[rows_of(k)],
                dst_ref=target.at[rows_of(k)],
                send_sem=send_sem.at[stream, k],
                recv_sem=recv_sem.at[stream, k],
                device_id=device,
                device_id_type=mesh_id,
            )

        return of

    def sum_copy(source, target, device):
        return pltpu.make_async_remote_copy(
            src_ref=sums.at[source],
            dst_ref=arrived.at[target],
            send_sem=sum_send_sem.at[target],
            recv_sem=sum_recv_sem.at[target],
            device_id=device,
            device_id_type=mesh_id,
        )

    totals[...] = jnp.zeros_like(totals)
    own_row, far_row = g * half_rows, (1 - g) * half_rows

    to_mate_a0 = copy(0, played_0, mate_a, mate)
    to_mate_a1 = copy(0, played_1, mate_a, mate)
    to_mate_b = copy(1, played_1, mate_b, mate)
    to_next_a = copy(2, played_1, guest_a, (next_2, 1 - g))
    to_back_a = copy(2, played_1, guest_a, (back_2, 1 - g))
    to_next_b = copy(3, played_0, guest_b, (next_1, 1 - g))
    to_core = copy(4, played_0, chip_guest.at[0], other_core)
    to_core_passed = copy(5, mate_a, chip_guest.at[1], other_core)

    load_plan.wait()
    load_counts.wait()
    slot_0, slot_1 = plan[0, m], plan[1, m]
    count_0, count_1 = counts[2 * m + slot_0], counts[2 * m + slot_1]
    guest_count_0 = counts[2 * back_1 + plan[0, back_1]]
    guest_1 = lax.rem(m + blk_count + 2 - 4 * core, blk_count)
    guest_count_1 = counts[2 * guest_1 + plan[1, guest_1]]

    pl.semaphore_wait(barrier, 3)

    @pl.when(core == 0)
    def _():
        pl.semaphore_signal(ready, inc=1, device_id=(next_2, 1 - g), device_id_type=mesh_id)

    for k in range(chunks):
        load(k).wait()
        here = rows_of(k)
        first, second = staged[0, here], staged[1, here]
        played_0[here, :] = jnp.where(slot_0 == 0, first, second)
        played_1[here, :] = jnp.where(slot_1 == 0, first, second)

        @pl.when(core == 0)
        def _():
            to_mate_a0(k).start()
            to_core(k).start()

        @pl.when(core == 1)
        def _():
            to_next_b(k).start()

    for k in range(chunks):

        @pl.when(core == 0)
        def _():
            to_mate_b(k).start()

        @pl.when(core == 1)
        def _():
            to_next_a(k).start()

    pair = 2 * chunk
    gate = chunks - 5

    def pair_of(i):
        return pl.ds(pl.multiple_of(i * pair, pair), pair)

    def put_norms(place, source, first, first_row, count, many=2):
        for k in range(many):
            rows = source[rows_of(first + k), :]
            norms[place, pl.ds(first + k, 1), :] = lane_norms(rows, first_row + (first + k) * chunk, count)

    def put_sums(place, first, values):
        for k in range(values.shape[1] // 128):
            sums[place, pl.ds(first + k, 1), :] = values[:, k * 128 : (k + 1) * 128]

    def arrive(stream, first, many=2):
        for k in range(many):
            stream(first + k).wait_recv()

    def own_norms(k, carry):
        put_norms(0, played_0, k, own_row, count_0, 1)
        put_norms(1, played_1, k, own_row, count_1, 1)
        return carry

    lax.fori_loop(0, chunks, own_norms, 0)

    def whole(rows, beside, resident, place):
        return tile_sums(rows, beside, resident, norms.at[place], totals.at[place])

    def store(density_0, density_1):
        places = lax.broadcasted_iota(jnp.int32, (chunks, 128), 0) * 128 + lax.broadcasted_iota(jnp.int32, (chunks, 128), 1)
        for slot in range(2):
            both = jnp.where(slot_0 == slot, density_0, 0.0) + jnp.where(slot_1 == slot, density_1, 0.0)
            both = jnp.where(own_row + places < counts[2 * m + slot], both, 0.0)
            for k in range(chunks):
                out[slot : slot + 1, k * 128 : (k + 1) * 128] = both[k : k + 1, :]

    @pl.when(core == 0)
    def _():
        def guests_of_round_0(i, carry):
            for k in range(2):
                to_mate_a0(2 * i + k).wait_recv()
                to_core_passed(2 * i + k).start()
            arrive(to_next_b, 2 * i)
            put_norms(2, guest_b, 2 * i, far_row, guest_count_0)
            rows = guest_b[pair_of(i), :]
            beside = column_norms(rows, far_row + i * pair, guest_count_0)
            put_sums(0, 2 * i, whole(rows, beside, played_0, 0))
            return carry

        lax.fori_loop(0, chunks // 2, guests_of_round_0, 0)

        def mates_of_round_0(i, carry):
            rows = mate_a[pair_of(i), :]
            beside = column_norms(rows, far_row + i * pair, count_0)
            put_sums(2, 2 * i, whole(rows, beside, guest_b, 2))
            return carry

        lax.fori_loop(0, chunks // 2, mates_of_round_0, 0)
        sums[0] += folded_rows(totals[2])
        sum_copy(0, 5, (back_1, 1 - g)).start()
        sum_copy(2, 0, mate).start()

        def mates_of_round_1(k, carry):
            to_mate_b(k).wait_recv()

            @pl.when(k == gate)
            def _():
                pl.semaphore_signal(turn, inc=1, device_id=other_core, device_id_type=mesh_id)
                pl.semaphore_wait(ready, 1)
                for every in range(chunks):
                    to_back_a(every).start()

            put_norms(3, mate_b, k, far_row, count_1, 1)
            return carry

        lax.fori_loop(0, chunks, mates_of_round_1, 0)

        def guests_of_round_1(first, many):
            arrive(to_back_a, first, many)
            rows = guest_a[pl.ds(pl.multiple_of(first * chunk, chunk), many * chunk), :]
            beside = column_norms(rows, far_row + first * chunk, guest_count_1)
            put_sums(1, first, whole(rows, beside, played_1, 1) + whole(rows, beside, mate_b, 3))

        def two_chunks(i, carry):
            guests_of_round_1(2 * i, 2)
            return carry

        lax.fori_loop(0, chunks // 2 - 1, two_chunks, 0)
        for k in range(chunks):
            for sent in (to_mate_a0, to_core, to_core_passed):
                sent(k).wait_send()
        for target in (0, 2, 3):
            sum_copy(0, target, mate).wait_recv()
        density_0 = folded_rows(totals[0]) + arrived[0] + arrived[2] + arrived[3]
        for k in (chunks - 2, chunks - 1):
            guests_of_round_1(k, 1)
        sum_copy(1, 4, (next_2, 1 - g)).start()
        sums[3] = folded_rows(totals[3])
        sum_copy(3, 1, mate).start()

        density_1 = folded_rows(totals[1])
        for k in range(chunks):
            for sent in (to_back_a, to_mate_b):
                sent(k).wait_send()
        for source, target in ((0, 5), (2, 0), (3, 1), (1, 4)):
            sum_copy(source, target, mate).wait_send()
        for target in (1, 4):
            sum_copy(0, target, mate).wait_recv()
        store(density_0, density_1 + arrived[1] + arrived[4])

    @pl.when(core == 1)
    def _():
        def near_half(i, carry):
            arrive(to_core, 2 * i)
            rows = chip_guest[0, pair_of(i), :]
            beside = column_norms(rows, own_row + i * pair, guest_count_0)
            put_sums(0, 2 * i, whole(rows, beside, played_0, 0))
            return carry

        lax.fori_loop(0, chunks // 2, near_half, 0)
        sum_copy(0, 2, other_core).start()

        def far_half(i, carry):
            arrive(to_core_passed, 2 * i)
            rows = chip_guest[1, pair_of(i), :]
            beside = column_norms(rows, far_row + i * pair, guest_count_0)
            put_sums(1, 2 * i, whole(rows, beside, played_0, 0))
            return carry

        lax.fori_loop(0, chunks // 2, far_half, 0)
        sum_copy(1, 3, (back_1, 1 - g)).start()

        def guests_of_round_1(i, carry):
            @pl.when(i == chunks // 2 - 2)
            def _():
                pl.semaphore_wait(turn, 1)
                for every in range(chunks):
                    to_mate_a1(every).start()

            arrive(to_next_a, 2 * i)
            put_norms(2, guest_a, 2 * i, far_row, guest_count_1)
            rows = guest_a[pair_of(i), :]
            beside = column_norms(rows, far_row + i * pair, guest_count_1)
            put_sums(2, 2 * i, whole(rows, beside, played_1, 1))
            return carry

        lax.fori_loop(0, chunks // 2, guests_of_round_1, 0)

        def mates_of_round_1(first, many):
            arrive(to_mate_a1, first, many)
            rows = mate_a[pl.ds(pl.multiple_of(first * chunk, chunk), many * chunk), :]
            beside = column_norms(rows, far_row + first * chunk, count_1)
            put_sums(3, first, whole(rows, beside, guest_a, 2))

        def two_chunks(i, carry):
            mates_of_round_1(2 * i, 2)
            return carry

        lax.fori_loop(0, chunks // 2 - 1, two_chunks, 0)
        for k in range(chunks):
            for sent in (to_next_a, to_next_b):
                sent(k).wait_send()
        sum_copy(0, 5, mate).wait_recv()
        density_0, density_1 = folded_rows(totals[0]) + arrived[5], folded_rows(totals[1])
        for k in (chunks - 2, chunks - 1):
            mates_of_round_1(k, 1)
        sums[2] += folded_rows(totals[2])
        sum_copy(2, 4, (back_2, 1 - g)).start()
        sum_copy(3, 1, mate).start()
        for k in range(chunks):
            to_mate_a1(k).wait_send()
        for source, target in ((0, 2), (1, 3), (2, 4), (3, 1)):
            sum_copy(source, target, mate).wait_send()
        for target in (1, 4):
            sum_copy(0, target, mate).wait_recv()
        store(density_0, density_1 + arrived[1] + arrived[4])


def on_device(embeddings, counts, plan):
    _, half_rows, width = embeddings.shape
    chunks = half_rows // chunk
    half_block = pltpu.VMEM((half_rows, width), embeddings.dtype)
    two_halves = pltpu.VMEM((2, half_rows, width), embeddings.dtype)
    return pl.pallas_call(
        functools.partial(kernel, lax.axis_size("blk")),
        out_shape=jax.ShapeDtypeStruct((2, half_rows), jnp.float32),
        in_specs=[
            pl.BlockSpec(memory_space=pltpu.HBM),
            pl.BlockSpec(memory_space=pltpu.HBM),
            pl.BlockSpec(memory_space=pltpu.HBM),
        ],
        out_specs=pl.BlockSpec(memory_space=pltpu.VMEM),
        scratch_shapes=[
            pltpu.SMEM(plan.shape[::-1], plan.dtype),
            pltpu.SMEM(counts.shape, counts.dtype),
            two_halves,
            half_block, half_block, half_block, half_block, half_block, half_block,
            two_halves,
            pltpu.VMEM((4, chunks, 128), jnp.float32),
            pltpu.VMEM((4, 8, half_rows), jnp.float32),
            pltpu.VMEM((4, chunks, 128), jnp.float32),
            pltpu.VMEM((6, chunks, 128), jnp.float32),
            pltpu.SemaphoreType.REGULAR,
            pltpu.SemaphoreType.REGULAR,
            pltpu.SemaphoreType.DMA((2,)),
            pltpu.SemaphoreType.DMA((chunks,)),
            pltpu.SemaphoreType.DMA((6, chunks)),
            pltpu.SemaphoreType.DMA((6, chunks)),
            pltpu.SemaphoreType.DMA((6,)),
            pltpu.SemaphoreType.DMA((6,)),
        ],
        compiler_params=pltpu.CompilerParams(
            collective_id=0, has_side_effects=True, vmem_limit_bytes=32 * 2**20
        ),
    )(*(pltpu.with_memory_space_constraint(operand, pltpu.HBM) for operand in (plan.T, counts, embeddings)))


def solution(mesh):
    return jax.shard_map(
        on_device,
        mesh=mesh,
        in_specs=(P("blk", "grp", None), P(), P()),
        out_specs=P("blk", "grp"),
        check_vma=False,
    )
```

time: 71.6 us -> 65.8 us (0.919)
  Pallas kernels: 70.1 us -> 65.1 us
    pallas_call x1, Pallas kernels: 70.1 us -> 65.1 us  [on_device(): pl.pallas_call(functools.partial(kernel, lax.axis_size('blk')), out_shape...]
where the time goes in v2:
time: 65.8 us; the launch traced here: 65.7 us
  Pallas kernels  65.1 us (99%)
    pallas_call x1, Pallas kernels, on_device(): pl.pallas_call(functools.partial(kernel, lax.axis_size('blk')), out_shape...  65.1 us

profile of v2, /device:TPU:1, one launch (start us, length us, event | category | flops | bytes accessed | tf_op | source)
XLA Modules:
  0.0 65.7 jit_solution(9870928714557051374)
XLA Ops:
  0.0 65.1 %shard_map.37 = f32[2,1024]{1,0:T(2,128)S(1)} custom-call(s32[2,128]{1,0:T(2,128)} %bitcast.1, s32[256]{0:T(256)} %counts_in_hbm.1, bf16[2,1024,768]{2,1,0:T(8,128)(2,1)} %embeddings.1), custom_call_target="tpu_custom_call" | custom-call | tf_op jit(solution)/shard_map/pallas_call | solution.py:346
  65.1 0.6 copy.5

commit v3 on v2

--- a/solution.py
+++ b/solution.py
@@ -59,6 +59,7 @@
     ready, turn, small_sem, staged_sem, send_sem, recv_sem, sum_send_sem, sum_recv_sem,
 ):
     half_rows = embeddings.shape[1]
+    ahead = 3
     chunks = half_rows // chunk
     m, g = lax.axis_index("blk"), lax.axis_index("grp")
     core = lax.rem(m, 2)
@@ -158,6 +159,12 @@
         @pl.when(core == 1)
         def _():
             to_next_a(k).start()
+
+    @pl.when(core == 0)
+    def _():
+        pl.semaphore_wait(ready, 1)
+        for early in range(ahead):
+            to_back_a(early).start()
 
     pair = 2 * chunk
     gate = chunks - 5
@@ -228,9 +235,8 @@
             @pl.when(k == gate)
             def _():
                 pl.semaphore_signal(turn, inc=1, device_id=other_core, device_id_type=mesh_id)
-                pl.semaphore_wait(ready, 1)
-                for every in range(chunks):
-                    to_back_a(every).start()
+                for late in range(ahead, chunks):
+                    to_back_a(late).start()
 
             put_norms(3, mate_b, k, far_row, count_1, 1)
             return carry
@@ -292,13 +298,13 @@
         lax.fori_loop(0, chunks // 2, far_half, 0)
         sum_copy(1, 3, (back_1, 1 - g)).start()
 
+        pl.semaphore_wait(turn, 1)
+        for k in range(chunks):
+            to_mate_a1(k).start()
+
+        early_rows = half_rows - pair
+
         def guests_of_round_1(i, carry):
-            @pl.when(i == chunks // 2 - 2)
-            def _():
-                pl.semaphore_wait(turn, 1)
-                for every in range(chunks):
-                    to_mate_a1(every).start()
-
             arrive(to_next_a, 2 * i)
             put_norms(2, guest_a, 2 * i, far_row, guest_count_1)
             rows = guest_a[pair_of(i), :]
@@ -306,31 +312,38 @@
             put_sums(2, 2 * i, whole(rows, beside, played_1, 1))
             return carry
 
-        lax.fori_loop(0, chunks // 2, guests_of_round_1, 0)
+        lax.fori_loop(0, chunks // 2 - 1, guests_of_round_1, 0)
 
         def mates_of_round_1(first, many):
             arrive(to_mate_a1, first, many)
+            put_norms(3, mate_a, first, far_row, count_1, many)
             rows = mate_a[pl.ds(pl.multiple_of(first * chunk, chunk), many * chunk), :]
             beside = column_norms(rows, far_row + first * chunk, count_1)
-            put_sums(3, first, whole(rows, beside, guest_a, 2))
+            put_sums(3, first, whole(rows, beside, guest_a.at[pl.ds(0, early_rows)], 2))
 
         def two_chunks(i, carry):
             mates_of_round_1(2 * i, 2)
             return carry
 
         lax.fori_loop(0, chunks // 2 - 1, two_chunks, 0)
+        sum_copy(0, 5, mate).wait_recv()
+        density_0 = folded_rows(totals[0]) + arrived[5]
         for k in range(chunks):
-            for sent in (to_next_a, to_next_b):
-                sent(k).wait_send()
-        sum_copy(0, 5, mate).wait_recv()
-        density_0, density_1 = folded_rows(totals[0]) + arrived[5], folded_rows(totals[1])
+            to_next_b(k).wait_send()
         for k in (chunks - 2, chunks - 1):
             mates_of_round_1(k, 1)
+        arrive(to_next_a, chunks - 2)
+        rows = guest_a[early_rows:half_rows, :]
+        beside = column_norms(rows, far_row + early_rows, guest_count_1)
+        put_sums(2, chunks - 2, whole(rows, beside, played_1, 1) + whole(rows, beside, mate_a, 3))
         sums[2] += folded_rows(totals[2])
         sum_copy(2, 4, (back_2, 1 - g)).start()
+        sums[3] += folded_rows(totals[3])
         sum_copy(3, 1, mate).start()
+        density_1 = folded_rows(totals[1])
         for k in range(chunks):
-            to_mate_a1(k).wait_send()
+            for sent in (to_next_a, to_mate_a1):
+                sent(k).wait_send()
         for source, target in ((0, 2), (1, 3), (2, 4), (3, 1)):
             sum_copy(source, target, mate).wait_send()
         for target in (1, 4):

time: 65.8 us -> 63.4 us (0.964)
  Pallas kernels: 65.1 us -> 62.4 us
    pallas_call x1, Pallas kernels: 65.1 us -> 62.4 us  [on_device(): pl.pallas_call(functools.partial(kernel, lax.axis_size('blk')), out_shape...]
where the time goes in v3:
time: 63.4 us; the launch traced here: 63 us
  Pallas kernels  62.4 us (98%)
    pallas_call x1, Pallas kernels, on_device(): pl.pallas_call(functools.partial(kernel, lax.axis_size('blk')), out_shape...  62.4 us

profile of v3, /device:TPU:1, one launch (start us, length us, event | category | flops | bytes accessed | tf_op | source)
XLA Modules:
  0.0 63.0 jit_solution(18378302022459489877)
XLA Ops:
  0.0 62.4 %shard_map.37 = f32[2,1024]{1,0:T(2,128)S(1)} custom-call(s32[2,128]{1,0:T(2,128)} %bitcast.1, s32[256]{0:T(256)} %counts_in_hbm.1, bf16[2,1024,768]{2,1,0:T(8,128)(2,1)} %embeddings.1), custom_call_target="tpu_custom_call" | custom-call | tf_op jit(solution)/shard_map/pallas_call | solution.py:359
  62.4 0.6 copy.5

commit v4 on v3

--- a/solution.py
+++ b/solution.py
@@ -30,13 +30,16 @@
     return jnp.where(row_ids < count, norms, jnp.inf)
 
 
-def tile_sums(rows, norms, resident, resident_norms, totals):
+def tile_sums(rows, norms, resident, resident_norms, totals, turned=False):
     height, width = rows.shape[0], 256
     row_part = jnp.zeros((height, 128), jnp.float32)
-    for start in range(0, resident.shape[0], width):
-        inner = lax.dot_general(
-            rows, resident[start : start + width, :], (((1,), (1,)), ((), ())), preferred_element_type=jnp.float32
-        )
+    for start in range(0, resident.shape[1 if turned else 0], width):
+        if turned:
+            inner = jnp.dot(rows, resident[:, start : start + width], preferred_element_type=jnp.float32)
+        else:
+            inner = lax.dot_general(
+                rows, resident[start : start + width, :], (((1,), (1,)), ((), ())), preferred_element_type=jnp.float32
+            )
         for left in range(0, width, 128):
             place = (start + left) // 128
             half_distance = (norms + resident_norms[place : place + 1, :]) - inner[:, left : left + 128]
@@ -54,7 +57,7 @@
 
 def kernel(
     blk_count, plan_in_hbm, counts_in_hbm, embeddings, out,
-    plan, counts, staged, played_0, played_1, mate_a, mate_b, guest_a, guest_b, chip_guest,
+    plan, counts, staged, played_0, played_1, mate_a, mate_b, guest_a, guest_b, chip_guest, turned_1, turned_mate,
     norms, totals, sums, arrived,
     ready, turn, small_sem, staged_sem, send_sem, recv_sem, sum_send_sem, sum_recv_sem,
 ):
@@ -167,7 +170,7 @@
             to_back_a(early).start()
 
     pair = 2 * chunk
-    gate = chunks - 5
+    turn_gate, back_gate = chunks - 3, chunks - 5
 
     def pair_of(i):
         return pl.ds(pl.multiple_of(i * pair, pair), pair)
@@ -188,12 +191,16 @@
     def own_norms(k, carry):
         put_norms(0, played_0, k, own_row, count_0, 1)
         put_norms(1, played_1, k, own_row, count_1, 1)
+        turned_1[:, rows_of(k)] = played_1[rows_of(k), :].T
         return carry
 
     lax.fori_loop(0, chunks, own_norms, 0)
 
     def whole(rows, beside, resident, place):
         return tile_sums(rows, beside, resident, norms.at[place], totals.at[place])
+
+    def whole_turned(rows, beside, resident, place):
+        return tile_sums(rows, beside, resident, norms.at[place], totals.at[place], True)
 
     def store(density_0, density_1):
         places = lax.broadcasted_iota(jnp.int32, (chunks, 128), 0) * 128 + lax.broadcasted_iota(jnp.int32, (chunks, 128), 1)
@@ -209,6 +216,11 @@
             for k in range(2):
                 to_mate_a0(2 * i + k).wait_recv()
                 to_core_passed(2 * i + k).start()
+
+            @pl.when(i == chunks // 2 - 1)
+            def _():
+                to_back_a(ahead).start()
+
             arrive(to_next_b, 2 * i)
             put_norms(2, guest_b, 2 * i, far_row, guest_count_0)
             rows = guest_b[pair_of(i), :]
@@ -232,13 +244,17 @@
         def mates_of_round_1(k, carry):
             to_mate_b(k).wait_recv()
 
-            @pl.when(k == gate)
+            @pl.when(k == turn_gate)
             def _():
                 pl.semaphore_signal(turn, inc=1, device_id=other_core, device_id_type=mesh_id)
-                for late in range(ahead, chunks):
+
+            @pl.when(k == back_gate)
+            def _():
+                for late in range(ahead + 1, chunks):
                     to_back_a(late).start()
 
             put_norms(3, mate_b, k, far_row, count_1, 1)
+            turned_mate[:, rows_of(k)] = mate_b[rows_of(k), :].T
             return carry
 
         lax.fori_loop(0, chunks, mates_of_round_1, 0)
@@ -247,7 +263,7 @@
             arrive(to_back_a, first, many)
             rows = guest_a[pl.ds(pl.multiple_of(first * chunk, chunk), many * chunk), :]
             beside = column_norms(rows, far_row + first * chunk, guest_count_1)
-            put_sums(1, first, whole(rows, beside, played_1, 1) + whole(rows, beside, mate_b, 3))
+            put_sums(1, first, whole_turned(rows, beside, turned_1, 1) + whole_turned(rows, beside, turned_mate, 3))
 
         def two_chunks(i, carry):
             guests_of_round_1(2 * i, 2)
@@ -317,6 +333,8 @@
         def mates_of_round_1(first, many):
             arrive(to_mate_a1, first, many)
             put_norms(3, mate_a, first, far_row, count_1, many)
+            for k in range(many):
+                turned_mate[:, rows_of(first + k)] = mate_a[rows_of(first + k), :].T
             rows = mate_a[pl.ds(pl.multiple_of(first * chunk, chunk), many * chunk), :]
             beside = column_norms(rows, far_row + first * chunk, count_1)
             put_sums(3, first, whole(rows, beside, guest_a.at[pl.ds(0, early_rows)], 2))
@@ -330,12 +348,19 @@
         density_0 = folded_rows(totals[0]) + arrived[5]
         for k in range(chunks):
             to_next_b(k).wait_send()
-        for k in (chunks - 2, chunks - 1):
-            mates_of_round_1(k, 1)
-        arrive(to_next_a, chunks - 2)
-        rows = guest_a[early_rows:half_rows, :]
-        beside = column_norms(rows, far_row + early_rows, guest_count_1)
-        put_sums(2, chunks - 2, whole(rows, beside, played_1, 1) + whole(rows, beside, mate_a, 3))
+        mates_of_round_1(chunks - 2, 1)
+
+        def last_guests(k):
+            to_next_a(k).wait_recv()
+            rows = guest_a[k * chunk : (k + 1) * chunk, :]
+            beside = column_norms(rows, far_row + k * chunk, guest_count_1)
+            return rows, beside, whole_turned(rows, beside, turned_1, 1)
+
+        rows, beside, near = last_guests(chunks - 2)
+        mates_of_round_1(chunks - 1, 1)
+        put_sums(2, chunks - 2, near + whole_turned(rows, beside, turned_mate, 3))
+        rows, beside, near = last_guests(chunks - 1)
+        put_sums(2, chunks - 1, near + whole_turned(rows, beside, turned_mate, 3))
         sums[2] += folded_rows(totals[2])
         sum_copy(2, 4, (back_2, 1 - g)).start()
         sums[3] += folded_rows(totals[3])
@@ -355,6 +380,7 @@
     _, half_rows, width = embeddings.shape
     chunks = half_rows // chunk
     half_block = pltpu.VMEM((half_rows, width), embeddings.dtype)
+    turned_block = pltpu.VMEM((width, half_rows), embeddings.dtype)
     two_halves = pltpu.VMEM((2, half_rows, width), embeddings.dtype)
     return pl.pallas_call(
         functools.partial(kernel, lax.axis_size("blk")),
@@ -371,6 +397,7 @@
             two_halves,
             half_block, half_block, half_block, half_block, half_block, half_block,
             two_halves,
+            turned_block, turned_block,
             pltpu.VMEM((4, chunks, 128), jnp.float32),
             pltpu.VMEM((4, 8, half_rows), jnp.float32),
             pltpu.VMEM((4, chunks, 128), jnp.float32),

time: 63.4 us -> 62.8 us (level)
  no operation moved by 1% of the time
where the time goes in v4:
time: 62.8 us; the launch traced here: 62.5 us
  Pallas kernels  61.9 us (99%)
    pallas_call x1, Pallas kernels, on_device(): pl.pallas_call(functools.partial(kernel, lax.axis_size('blk')), out_shape...  61.9 us

profile of v4, /device:TPU:1, one launch (start us, length us, event | category | flops | bytes accessed | tf_op | source)
XLA Modules:
  0.0 62.5 jit_solution(12280720334088327014)
XLA Ops:
  0.0 61.9 %shard_map.37 = f32[2,1024]{1,0:T(2,128)S(1)} custom-call(s32[2,128]{1,0:T(2,128)} %bitcast.1, s32[256]{0:T(256)} %counts_in_hbm.1, bf16[2,1024,768]{2,1,0:T(8,128)(2,1)} %embeddings.1), custom_call_target="tpu_custom_call" | custom-call | tf_op jit(solution)/shard_map/pallas_call | solution.py:385
  61.9 0.6 copy.5

commit v5 on v4

--- a/solution.py
+++ b/solution.py
@@ -57,7 +57,7 @@
 
 def kernel(
     blk_count, plan_in_hbm, counts_in_hbm, embeddings, out,
-    plan, counts, staged, played_0, played_1, mate_a, mate_b, guest_a, guest_b, chip_guest, turned_1, turned_mate,
+    plan, counts, staged, played_0, played_1, mate_a, mate_b, guest_a, guest_b, chip_guest, turned_1, turned_mate, turned_guest,
     norms, totals, sums, arrived,
     ready, turn, small_sem, staged_sem, send_sem, recv_sem, sum_send_sem, sum_recv_sem,
 ):
@@ -323,6 +323,8 @@
         def guests_of_round_1(i, carry):
             arrive(to_next_a, 2 * i)
             put_norms(2, guest_a, 2 * i, far_row, guest_count_1)
+            for k in range(2):
+                turned_guest[:, rows_of(2 * i + k)] = guest_a[rows_of(2 * i + k), :].T
             rows = guest_a[pair_of(i), :]
             beside = column_norms(rows, far_row + i * pair, guest_count_1)
             put_sums(2, 2 * i, whole(rows, beside, played_1, 1))
@@ -337,7 +339,7 @@
                 turned_mate[:, rows_of(first + k)] = mate_a[rows_of(first + k), :].T
             rows = mate_a[pl.ds(pl.multiple_of(first * chunk, chunk), many * chunk), :]
             beside = column_norms(rows, far_row + first * chunk, count_1)
-            put_sums(3, first, whole(rows, beside, guest_a.at[pl.ds(0, early_rows)], 2))
+            put_sums(3, first, whole_turned(rows, beside, turned_guest.at[:, pl.ds(0, early_rows)], 2))
 
         def two_chunks(i, carry):
             mates_of_round_1(2 * i, 2)
@@ -359,9 +361,9 @@
         rows, beside, near = last_guests(chunks - 2)
         mates_of_round_1(chunks - 1, 1)
         put_sums(2, chunks - 2, near + whole_turned(rows, beside, turned_mate, 3))
+        sums[2] += folded_rows(totals[2])
         rows, beside, near = last_guests(chunks - 1)
         put_sums(2, chunks - 1, near + whole_turned(rows, beside, turned_mate, 3))
-        sums[2] += folded_rows(totals[2])
         sum_copy(2, 4, (back_2, 1 - g)).start()
         sums[3] += folded_rows(totals[3])
         sum_copy(3, 1, mate).start()
@@ -397,7 +399,7 @@
             two_halves,
             half_block, half_block, half_block, half_block, half_block, half_block,
             two_halves,
-            turned_block, turned_block,
+            turned_block, turned_block, turned_block,
             pltpu.VMEM((4, chunks, 128), jnp.float32),
             pltpu.VMEM((4, 8, half_rows), jnp.float32),
             pltpu.VMEM((4, chunks, 128), jnp.float32),

time: 62.8 us -> 62.8 us (level)
  no operation moved by 1% of the time
where the time goes in v5:
time: 62.8 us; the launch traced here: 62.3 us
  Pallas kernels  61.7 us (98%)
    pallas_call x1, Pallas kernels, on_device(): pl.pallas_call(functools.partial(kernel, lax.axis_size('blk')), out_shape...  61.7 us

profile of v5, /device:TPU:1, one launch (start us, length us, event | category | flops | bytes accessed | tf_op | source)
XLA Modules:
  0.0 62.3 jit_solution(2663072709216117711)
XLA Ops:
  0.0 61.7 %shard_map.37 = f32[2,1024]{1,0:T(2,128)S(1)} custom-call(s32[2,128]{1,0:T(2,128)} %bitcast.1, s32[256]{0:T(256)} %counts_in_hbm.1, bf16[2,1024,768]{2,1,0:T(8,128)(2,1)} %embeddings.1), custom_call_target="tpu_custom_call" | custom-call | tf_op jit(solution)/shard_map/pallas_call | solution.py:387
  61.7 0.6 copy.5

commit v6 on v4

--- a/solution.py
+++ b/solution.py
@@ -276,11 +276,15 @@
         for target in (0, 2, 3):
             sum_copy(0, target, mate).wait_recv()
         density_0 = folded_rows(totals[0]) + arrived[0] + arrived[2] + arrived[3]
-        for k in (chunks - 2, chunks - 1):
-            guests_of_round_1(k, 1)
-        sum_copy(1, 4, (next_2, 1 - g)).start()
+        guests_of_round_1(chunks - 2, 1)
+        to_back_a(chunks - 1).wait_recv()
+        rows = guest_a[half_rows - chunk : half_rows, :]
+        beside = column_norms(rows, far_row + half_rows - chunk, guest_count_1)
+        far = whole_turned(rows, beside, turned_mate, 3)
         sums[3] = folded_rows(totals[3])
         sum_copy(3, 1, mate).start()
+        put_sums(1, chunks - 1, far + whole_turned(rows, beside, turned_1, 1))
+        sum_copy(1, 4, (next_2, 1 - g)).start()
 
         density_1 = folded_rows(totals[1])
         for k in range(chunks):

time: 62.8 us -> 62.9 us (level)
  no operation moved by 1% of the time
where the time goes in v6:
time: 62.9 us; the launch traced here: 62.5 us
  Pallas kernels  61.9 us (98%)
    pallas_call x1, Pallas kernels, on_device(): pl.pallas_call(functools.partial(kernel, lax.axis_size('blk')), out_shape...  61.9 us

profile of v6, /device:TPU:1, one launch (start us, length us, event | category | flops | bytes accessed | tf_op | source)
XLA Modules:
  0.0 62.5 jit_solution(6129682066164455108)
XLA Ops:
  0.0 61.9 %shard_map.37 = f32[2,1024]{1,0:T(2,128)S(1)} custom-call(s32[2,128]{1,0:T(2,128)} %bitcast.1, s32[256]{0:T(256)} %counts_in_hbm.1, bf16[2,1024,768]{2,1,0:T(8,128)(2,1)} %embeddings.1), custom_call_target="tpu_custom_call" | custom-call | tf_op jit(solution)/shard_map/pallas_call | solution.py:389
  61.9 0.6 copy.5
